TPU v7x, 256 devices: a whole 4x4x8 slice. The times are simulated.
256 devices in a mesh: row: 4 (over y), col: 2 (over z_lo), depth: 32 (over z_hi, x, core).
Axes of the slice: x: 4, y: 4, z: 8 (z_hi: 4, z_lo: 2; z = z_hi * 2 + z_lo), core: 2. Of those that a mesh axis runs over, the one named last changes fastest.
Arguments:
- inputs: bfloat16 [1024, 12288], P(('col', 'depth'), 'row'), may hold values from -6 to 6
- weight: bfloat16 [12288, 49152], P('row', ('col', 'depth')), may hold values from -0.0546875 to 0.0546875
- out_grad: bfloat16 [1024, 49152], P('row', ('col', 'depth')), may hold values from -16 to 16
Outputs:
- activated: bfloat16 [1024, 49152], P('row', ('col', 'depth'))
- input_grad: bfloat16 [1024, 12288], P(('col', 'depth'), 'row')
- weight_grad: bfloat16 [12288, 49152], P('row', ('col', 'depth'))
All inputs are finite; a program needn't handle non-finite values.
Results may differ from a plain program's by a relative error of at most 0.0049.
Values may be sent and summed in bfloat16 or wider, within the bound.
No kernel may reach another device: no remote copies, remote signals or barrier semaphores. Data moves between devices by JAX's collectives and lax.ppermute only.
A program may use at most 128 MiB of HBM per device.

v0:
```python
import math
import jax
import jax.numpy as jnp
from jax import lax
from jax.sharding import PartitionSpec as P

gelu_coef = 0.044715


def gelu_pair(pre, cotangent):
    scale = math.sqrt(2.0 / math.pi)
    inner = scale * (pre + gelu_coef * pre * pre * pre)
    tanh_val = jnp.tanh(inner)
    activated = (0.5 * pre * (1.0 + tanh_val)).astype(jnp.bfloat16)
    slope = 0.5 * (1.0 + tanh_val) + 0.5 * pre * (1.0 - tanh_val * tanh_val) * scale * (
        1.0 + 3.0 * gelu_coef * pre * pre
    )
    pre_grad = (cotangent.astype(jnp.float32) * slope).astype(jnp.bfloat16)
    return (activated, pre_grad)


def body(inputs, weight, out_grad):
    gathered = lax.all_gather(inputs, ("col", "depth"), axis=0, tiled=True)
    partial_pre = jnp.dot(gathered, weight, preferred_element_type=jnp.float32)
    pre = lax.psum_scatter(partial_pre, "row", scatter_dimension=0, tiled=True)
    activated, pre_grad = gelu_pair(pre, out_grad)
    grad_all = lax.all_gather(pre_grad, "row", axis=0, tiled=True)
    weight_grad = lax.dot_general(
        gathered, grad_all, (((0,), (0,)), ((), ())), preferred_element_type=jnp.float32
    ).astype(jnp.bfloat16)
    input_grad = lax.psum_scatter(
        lax.dot_general(
            grad_all, weight, (((1,), (1,)), ((), ())), preferred_element_type=jnp.float32
        ),
        ("col", "depth"),
        scatter_dimension=0,
        tiled=True,
    )
    return (activated, input_grad.astype(jnp.bfloat16), weight_grad)


def solution(mesh):
    return jax.shard_map(
        body,
        mesh=mesh,
        in_specs=(
            P(("col", "depth"), "row"),
            P("row", ("col", "depth")),
            P("row", ("col", "depth")),
        ),
        out_specs=(
            P("row", ("col", "depth")),
            P(("col", "depth"), "row"),
            P("row", ("col", "depth")),
        ),
        check_vma=False,
    )
```

profile of v0, /device:TPU:48, one launch (start us, length us, event | category | flops | bytes accessed | tf_op | source)
XLA Modules:
  0.0 575.5 jit_solution(2355312599847938495)
XLA Ops:
  7.2 0.0 all-gather.3.cloned.1.call-start
  7.2 0.7 all-gather.3.cloned.1.call-update
  7.9 0.0 copy-start
  7.9 0.0 reduce-scatter.3.cloned.1.call-start
  8.0 122.7 %all-gather.3.cloned.1.call-done = bf16[1024,3072]{1,0:T(8,128)(2,1)} async-done(((bf16[16,3072]{1,0:T(8,128)(2,1)}), bf16[1024,3072]{1,0:T(8,128)(2,1)}) %all-gather.3.cloned.1.call-update) | async-done | bytes 6291472 | tf_op jit(solution)/shard_map/all_gather | solution.py:23
  130.7 9.6 %fusion.8 = f32[1024,768]{1,0:T(8,128)} fusion(bf16[1024,3072]{1,0:T(8,128)(2,1)} %all-gather.3.cloned.1.call-done, bf16[3072,768]{1,0:T(8,128)(2,1)} %param.4), kind=kOutput, calls=%fused_computation.12 | convolution fusion | flops 4831838208 | bytes 14155776 | tf_op jit(solution)/shard_map/dot_general | solution.py:24
  140.3 0.0 reduce-scatter.3.cloned.1.call-update
  140.4 0.0 all-gather.5.cloned.1.call-start
  140.4 37.5 %reduce-scatter.3.cloned.1.call-done = f32[256,768]{1,0:T(8,128)} async-done(((f32[1024,768]{1,0:T(8,128)}), f32[256,768]{1,0:T(8,128)}) %reduce-scatter.3.cloned.1.call-update) | async-done | bytes 786448 | tf_op jit(solution)/shard_map/reduce_scatter | solution.py:25
  178.0 0.0 copy-done
  178.0 2.6 fusion.7
  180.5 0.0 all-gather.5.cloned.1.call-update
  180.6 0.0 reduce-scatter.5.cloned.1.call-start
  180.6 29.3 %all-gather.5.cloned.1.call-done = bf16[1024,768]{1,0:T(8,128)(2,1)} async-done(((bf16[256,768]{1,0:T(8,128)(2,1)}), bf16[1024,768]{1,0:T(8,128)(2,1)}) %all-gather.5.cloned.1.call-update) | async-done | bytes 1572880 | tf_op jit(solution)/shard_map/all_gather | solution.py:27
  209.9 10.1 %fusion.9 = f32[1024,3072]{1,0:T(8,128)} fusion(bf16[1024,768]{1,0:T(8,128)(2,1)} %all-gather.5.cloned.1.call-done, bf16[3072,768]{1,0:T(8,128)(2,1)} %param.4), kind=kOutput, calls=%fused_computation.13 | convolution fusion | flops 4831838208 | bytes 18874368 | tf_op jit(solution)/shard_map/dot_general | solution.py:32
  220.0 0.0 copy-start.1
  220.0 0.0 reduce-scatter.5.cloned.1.call-update
  220.0 1.4 copy-done.1
  221.4 9.6 %fusion = bf16[3072,768]{0,1:T(8,128)(2,1)} fusion(bf16[1024,768]{1,0:T(8,128)(2,1)S(1)} %copy-done.1, bf16[1024,3072]{1,0:T(8,128)(2,1)} %all-gather.3.cloned.1.call-done), kind=kOutput, calls=%fused_computation.1 | convolution fusion | flops 4834197504 | bytes 12582912 | tf_op jit(solution)/shard_map/dot_general | solution.py:28
  231.0 6.6 %copy.6 = bf16[3072,768]{1,0:T(8,128)(2,1)} copy(bf16[3072,768]{0,1:T(8,128)(2,1)} %fusion) | data formatting | bytes 9437184
  237.6 329.8 %reduce-scatter.5.cloned.1.call-done = f32[16,3072]{1,0:T(8,128)} async-done(((f32[1024,3072]{1,0:T(8,128)}), f32[16,3072]{1,0:T(8,128)}) %reduce-scatter.5.cloned.1.call-update) | async-done | bytes 196624 | tf_op jit(solution)/shard_map/reduce_scatter | solution.py:31
  567.4 1.6 convert_element_type.21
Async XLA Ops:
  7.2 123.5 %all-gather.3.cloned.1.call-start = ((), (), s32[]{:S(2)}) async-start(), calls=%async_computation.2 | async-start | bytes 6389760 | tf_op jit(solution)/shard_map/all_gather | solution.py:23
  7.9 170.1 %copy-start = (bf16[256,768]{1,0:T(8,128)(2,1)S(1)}, bf16[256,768]{1,0:T(8,128)(2,1)}, u32[]{:S(2)}) copy-start(bf16[256,768]{1,0:T(8,128)(2,1)} %param.5) | copy-start | bytes 1179652
  7.9 170.0 %reduce-scatter.3.cloned.1.call-start = ((), (), s32[]{:S(2)}) async-start(), calls=%async_computation.3 | async-start | bytes 3932160 | tf_op jit(solution)/shard_map/reduce_scatter | solution.py:25
  140.4 69.5 %all-gather.5.cloned.1.call-start = ((), (), s32[]{:S(2)}) async-start(), calls=%async_computation.4 | async-start | bytes 1966080 | tf_op jit(solution)/shard_map/all_gather | solution.py:27
  180.6 386.9 %reduce-scatter.5.cloned.1.call-start = ((), (), s32[]{:S(2)}) async-start(), calls=%async_computation.5 | async-start | bytes 12779520 | tf_op jit(solution)/shard_map/reduce_scatter | solution.py:31
  220.0 1.4 copy-start.1
Sparse Core Ops, SparseCore 0:
  9.9 120.7 all-gather.2
  140.5 37.4 reduce-scatter.2
  180.7 29.1 all-gather.4
  220.2 347.2 reduce-scatter.4
where the time goes:
time: 576 us
  waiting for transfers between devices  520 us (90%)
  matrix products  29.4 us (5%)
  between operations  13.8 us (2%)
  local copies, waits for them, and re-layouts  8 us (1%)
    reduce_scatter x1, waiting for transfers between devices, body(): lax.psum_scatter(lax.dot_general(grad_all, weight, (((1,), (1,)), ((), ()...  330 us
    all_gather x1, waiting for transfers between devices, body(): gathered = lax.all_gather(inputs, ('col', 'depth'), axis=0, tiled=True)  123 us
    reduce_scatter x1, waiting for transfers between devices, body(): pre = lax.psum_scatter(partial_pre, 'row', scatter_dimension=0, tiled=True)  37.5 us
    all_gather x1, waiting for transfers between devices, body(): grad_all = lax.all_gather(pre_grad, 'row', axis=0, tiled=True)  29.3 us
  transfers between devices with their start and end apart: 4, of which 4 were waited for; matrix products, arithmetic and copies ran while one was open for 3% of the time, Pallas kernels for 0%

commit v1 on v0

--- a/solution.py
+++ b/solution.py
@@ -5,6 +5,14 @@
 from jax.sharding import PartitionSpec as P
 
 gelu_coef = 0.044715
+
+
+def gather_by_exchange(shard, axis, dim):
+    devices = lax.axis_size(axis)
+    repeats = [devices if d == dim else 1 for d in range(shard.ndim)]
+    return lax.all_to_all(
+        jnp.tile(shard, repeats), axis, split_axis=dim, concat_axis=dim, tiled=True
+    )
 
 
 def gelu_pair(pre, cotangent):
@@ -24,7 +32,7 @@
     partial_pre = jnp.dot(gathered, weight, preferred_element_type=jnp.float32)
     pre = lax.psum_scatter(partial_pre, "row", scatter_dimension=0, tiled=True)
     activated, pre_grad = gelu_pair(pre, out_grad)
-    grad_all = lax.all_gather(pre_grad, "row", axis=0, tiled=True)
+    grad_all = gather_by_exchange(pre_grad, "row", 0)
     weight_grad = lax.dot_general(
         gathered, grad_all, (((0,), (0,)), ((), ())), preferred_element_type=jnp.float32
     ).astype(jnp.bfloat16)

time: 576 us -> 567 us (0.984)
  waiting for transfers between devices: 520 us -> 491 us
  blocking collectives: 0 us -> 22.8 us
    all_gather x1 -> x0, waiting for transfers between devices: 29.3 us -> none  [body(): grad_all = lax.all_gather(pre_grad, 'row', axis=0, tiled=True)]
    all_to_all x0 -> x1, blocking collectives: none -> 22.8 us  [gather_by_exchange(): lax.all_to_all(jnp.tile(shard, repeats), axis, split_axis=dim, concat_axi...]
  transfers between devices with their start and end apart: 4 -> 3, of which waited for: 4 -> 3; matrix products, arithmetic and copies ran while one was open for 3% -> 3% of each run, Pallas kernels for 0% -> 0%
where the time goes in v1:
time: 567 us; the launch traced here: 566 us
  waiting for transfers between devices  491 us (87%)
  matrix products  27.2 us (5%)
  blocking collectives  22.8 us (4%)
  between operations  13.8 us (2%)
  local copies, waits for them, and re-layouts  6.72 us (1%)
    reduce_scatter x1, waiting for transfers between devices, body(): lax.psum_scatter(lax.dot_general(grad_all, weight, (((1,), (1,)), ((), ()...  330 us
    all_gather x1, waiting for transfers between devices, body(): gathered = lax.all_gather(inputs, ('col', 'depth'), axis=0, tiled=True)  123 us
    reduce_scatter x1, waiting for transfers between devices, body(): pre = lax.psum_scatter(partial_pre, 'row', scatter_dimension=0, tiled=True)  37.5 us
    all_to_all x1, blocking collectives, gather_by_exchange(): lax.all_to_all(jnp.tile(shard, repeats), axis, split_axis=dim, concat_axi...  22.8 us
  transfers between devices with their start and end apart: 3, of which 3 were waited for; matrix products, arithmetic and copies ran while one was open for 3% of the time, Pallas kernels for 0%

profile of v1, /device:TPU:48, one launch (start us, length us, event | category | flops | bytes accessed | tf_op | source)
XLA Modules:
  0.0 565.6 jit_solution(5045909330582475289)
XLA Ops:
  7.2 0.0 all-gather.2.cloned.1.call-start
  7.2 0.7 all-gather.2.cloned.1.call-update
  7.9 0.0 copy-start
  7.9 0.0 reduce-scatter.3.cloned.1.call-start
  8.0 122.7 %all-gather.2.cloned.1.call-done = bf16[1024,3072]{1,0:T(8,128)(2,1)} async-done(((bf16[16,3072]{1,0:T(8,128)(2,1)}), bf16[1024,3072]{1,0:T(8,128)(2,1)}) %all-gather.2.cloned.1.call-update) | async-done | bytes 6291472 | tf_op jit(solution)/shard_map/all_gather | solution.py:31
  130.7 9.6 %fusion.8 = f32[1024,768]{1,0:T(8,128)} fusion(bf16[1024,3072]{1,0:T(8,128)(2,1)} %all-gather.2.cloned.1.call-done, bf16[3072,768]{1,0:T(8,128)(2,1)} %param.4), kind=kOutput, calls=%fused_computation.12 | convolution fusion | flops 4831838208 | bytes 14155776 | tf_op jit(solution)/shard_map/dot_general | solution.py:32
  140.3 0.0 reduce-scatter.3.cloned.1.call-update
  140.4 0.0 reduce-scatter.5.cloned.1.call-start
  140.4 37.5 %reduce-scatter.3.cloned.1.call-done = f32[256,768]{1,0:T(8,128)} async-done(((f32[1024,768]{1,0:T(8,128)}), f32[256,768]{1,0:T(8,128)}) %reduce-scatter.3.cloned.1.call-update) | async-done | bytes 786448 | tf_op jit(solution)/shard_map/reduce_scatter | solution.py:33
  178.0 0.0 copy-done
  178.0 0.0 copy-start.1
  178.0 2.6 fusion.7
  180.5 0.1 tile.2
  180.7 22.8 %all_to_all.9 = bf16[4,256,768]{2,1,0:T(8,128)(2,1)S(1)} all-to-all(bf16[4,256,768]{2,1,0:T(8,128)(2,1)S(1)} %tile.2), channel_id=1, replica_groups=mesh['row'=4,'col'=2,'depth'=32] {'row'}, dimensions={0} | all-to-all | bytes 3145728 | tf_op jit(solution)/shard_map/all_to_all | solution.py:13
  203.5 0.0 copy-done.1
  203.5 7.9 %fusion.9 = f32[1024,3072]{1,0:T(8,128)} fusion(bf16[1024,768]{1,0:T(8,128)(2,1)S(1)} %bitcast.9, bf16[3072,768]{1,0:T(8,128)(2,1)S(1)} %copy-done.1), kind=kOutput, calls=%fused_computation.13 | convolution fusion | flops 4831838208 | bytes 18874368 | tf_op jit(solution)/shard_map/dot_general | solution.py:40
  211.4 0.0 reduce-scatter.5.cloned.1.call-update
  211.4 9.6 %fusion = bf16[3072,768]{0,1:T(8,128)(2,1)} fusion(bf16[1024,768]{1,0:T(8,128)(2,1)S(1)} %bitcast.10, bf16[1024,3072]{1,0:T(8,128)(2,1)} %all-gather.2.cloned.1.call-done), kind=kOutput, calls=%fused_computation.1 | convolution fusion | flops 4834197504 | bytes 12582912 | tf_op jit(solution)/shard_map/dot_general | solution.py:36
  221.0 6.6 %copy.6 = bf16[3072,768]{1,0:T(8,128)(2,1)} copy(bf16[3072,768]{0,1:T(8,128)(2,1)} %fusion) | data formatting | bytes 9437184
  227.6 329.8 %reduce-scatter.5.cloned.1.call-done = f32[16,3072]{1,0:T(8,128)} async-done(((f32[1024,3072]{1,0:T(8,128)}), f32[16,3072]{1,0:T(8,128)}) %reduce-scatter.5.cloned.1.call-update) | async-done | bytes 196624 | tf_op jit(solution)/shard_map/reduce_scatter | solution.py:39
  557.5 1.6 convert_element_type.21
Async XLA Ops:
  7.2 123.5 %all-gather.2.cloned.1.call-start = ((), (), s32[]{:S(2)}) async-start(), calls=%async_computation.3 | async-start | bytes 6389760 | tf_op jit(solution)/shard_map/all_gather | solution.py:31
  7.9 170.1 %copy-start = (bf16[256,768]{1,0:T(8,128)(2,1)S(1)}, bf16[256,768]{1,0:T(8,128)(2,1)}, u32[]{:S(2)}) copy-start(bf16[256,768]{1,0:T(8,128)(2,1)} %param.5) | copy-start | bytes 1179652
  7.9 170.0 %reduce-scatter.3.cloned.1.call-start = ((), (), s32[]{:S(2)}) async-start(), calls=%async_computation.4 | async-start | bytes 3932160 | tf_op jit(solution)/shard_map/reduce_scatter | solution.py:33
  140.4 417.1 %reduce-scatter.5.cloned.1.call-start = ((), (), s32[]{:S(2)}) async-start(), calls=%async_computation.5 | async-start | bytes 12779520 | tf_op jit(solution)/shard_map/reduce_scatter | solution.py:39
  178.0 25.5 %copy-start.1 = (bf16[3072,768]{1,0:T(8,128)(2,1)S(1)}, bf16[3072,768]{1,0:T(8,128)(2,1)}, u32[]{:S(2)}) copy-start(bf16[3072,768]{1,0:T(8,128)(2,1)} %param.4) | copy-start | bytes 14155780
Sparse Core Ops, SparseCore 0:
  9.9 120.7 all-gather.1
  140.5 37.4 reduce-scatter.2
  211.6 345.8 reduce-scatter.4

commit v2 on v0

--- a/solution.py
+++ b/solution.py
@@ -20,7 +20,12 @@
 
 
 def body(inputs, weight, out_grad):
-    gathered = lax.all_gather(inputs, ("col", "depth"), axis=0, tiled=True)
+    gathered = jnp.concatenate(
+        lax.all_to_all(
+            jnp.stack([inputs] * lax.axis_size(("col", "depth"))), ("col", "depth"), 0, 0
+        ),
+        axis=0,
+    )
     partial_pre = jnp.dot(gathered, weight, preferred_element_type=jnp.float32)
     pre = lax.psum_scatter(partial_pre, "row", scatter_dimension=0, tiled=True)
     activated, pre_grad = gelu_pair(pre, out_grad)

time: 576 us -> 606 us (1.052)
  blocking collectives: 0 us -> 152 us
  waiting for transfers between devices: 520 us -> 394 us
    all_to_all x0 -> x1, blocking collectives: none -> 152 us  [body(): lax.all_to_all(jnp.stack([inputs] * lax.axis_size(('col', 'depth'))), ('c...]
    all_gather x1 -> x0, waiting for transfers between devices: 123 us -> none  [body(): gathered = lax.all_gather(inputs, ('col', 'depth'), axis=0, tiled=True)]
  transfers between devices with their start and end apart: 4 -> 3, of which waited for: 4 -> 3; matrix products, arithmetic and copies ran while one was open for 3% -> 3% of each run, Pallas kernels for 0% -> 0%
where the time goes in v2:
time: 606 us; the launch traced here: 604 us
  waiting for transfers between devices  394 us (65%)
  blocking collectives  152 us (25%)
  matrix products  26.3 us (4%)
  between operations  13.8 us (2%)
  local copies, waits for them, and re-layouts  12.4 us (2%)
    reduce_scatter x1, waiting for transfers between devices, body(): lax.psum_scatter(lax.dot_general(grad_all, weight, (((1,), (1,)), ((), ()...  329 us
    all_to_all x1, blocking collectives, body(): lax.all_to_all(jnp.stack([inputs] * lax.axis_size(('col', 'depth'))), ('c...  152 us
    reduce_scatter x1, waiting for transfers between devices, body(): pre = lax.psum_scatter(partial_pre, 'row', scatter_dimension=0, tiled=True)  36.4 us
    all_gather x1, waiting for transfers between devices, body(): grad_all = lax.all_gather(pre_grad, 'row', axis=0, tiled=True)  29.3 us
  transfers between devices with their start and end apart: 3, of which 3 were waited for; matrix products, arithmetic and copies ran while one was open for 3% of the time, Pallas kernels for 0%

profile of v2, /device:TPU:48, one launch (start us, length us, event | category | flops | bytes accessed | tf_op | source)
XLA Modules:
  0.0 603.6 jit_solution(3068397853969887188)
XLA Ops:
  7.2 0.0 reduce-scatter.3.cloned.1.call-start
  7.2 0.0 slice-start
  7.2 1.8 stack.2
  9.0 0.0 slice-start.1
  9.1 152.3 %all_to_all.5 = bf16[64,16,3072]{2,1,0:T(8,128)(2,1)S(1)} all-to-all(bf16[64,16,3072]{2,1,0:T(8,128)(2,1)S(1)} %stack.2), channel_id=1, replica_groups=mesh['row'=4,'col'=2,'depth'=32] {'col','depth'}, dimensions={0} | all-to-all | bytes 12582912 | tf_op jit(solution)/shard_map/all_to_all | solution.py:24
  161.4 0.0 copy-start
  161.4 2.6 copy-done
  164.0 0.0 slice-done
  164.0 0.0 slice-done.1
  164.0 0.0 copy-start.1
  164.0 6.7 %fusion.8 = f32[1024,768]{1,0:T(8,128)} fusion(bf16[1024,3072]{1,0:T(8,128)(2,1)S(1)} %bitcast.9, bf16[3072,768]{1,0:T(8,128)(2,1)S(1)} %bitcast.12), kind=kOutput, calls=%fused_computation.12 | convolution fusion | flops 4831838208 | bytes 14155776 | tf_op jit(solution)/shard_map/dot_general | solution.py:29
  170.7 0.0 reduce-scatter.3.cloned.1.call-update
  170.7 0.0 all-gather.2.cloned.1.call-start
  170.8 36.4 %reduce-scatter.3.cloned.1.call-done = f32[256,768]{1,0:T(8,128)} async-done(((f32[1024,768]{1,0:T(8,128)}), f32[256,768]{1,0:T(8,128)}) %reduce-scatter.3.cloned.1.call-update) | async-done | bytes 786448 | tf_op jit(solution)/shard_map/reduce_scatter | solution.py:30
  207.2 0.0 copy-done.1
  207.2 2.6 fusion.7
  209.7 0.0 all-gather.2.cloned.1.call-update
  209.8 0.0 reduce-scatter.5.cloned.1.call-start
  209.8 29.3 %all-gather.2.cloned.1.call-done = bf16[1024,768]{1,0:T(8,128)(2,1)} async-done(((bf16[256,768]{1,0:T(8,128)(2,1)}), bf16[1024,768]{1,0:T(8,128)(2,1)}) %all-gather.2.cloned.1.call-update) | async-done | bytes 1572880 | tf_op jit(solution)/shard_map/all_gather | solution.py:32
  239.1 10.0 %fusion.9 = f32[1024,3072]{1,0:T(8,128)} fusion(bf16[1024,768]{1,0:T(8,128)(2,1)} %all-gather.2.cloned.1.call-done, bf16[3072,768]{1,0:T(8,128)(2,1)} %param.4), kind=kOutput, calls=%fused_computation.13 | convolution fusion | flops 4831838208 | bytes 18874368 | tf_op jit(solution)/shard_map/dot_general | solution.py:37
  249.2 0.0 copy-start.2
  249.2 0.0 reduce-scatter.5.cloned.1.call-update
  249.2 1.4 copy-done.2
  250.6 9.6 %fusion = bf16[3072,768]{0,1:T(8,128)(2,1)} fusion(bf16[1024,768]{1,0:T(8,128)(2,1)S(1)} %copy-done.2, bf16[1024,3072]{1,0:T(8,128)(2,1)} %bitcast.10), kind=kOutput, calls=%fused_computation.1 | convolution fusion | flops 4834197504 | bytes 12582912 | tf_op jit(solution)/shard_map/dot_general | solution.py:33
  260.2 6.6 %copy.6 = bf16[3072,768]{1,0:T(8,128)(2,1)} copy(bf16[3072,768]{0,1:T(8,128)(2,1)} %fusion) | data formatting | bytes 9437184
  266.8 328.7 %reduce-scatter.5.cloned.1.call-done = f32[16,3072]{1,0:T(8,128)} async-done(((f32[1024,3072]{1,0:T(8,128)}), f32[16,3072]{1,0:T(8,128)}) %reduce-scatter.5.cloned.1.call-update) | async-done | bytes 196624 | tf_op jit(solution)/shard_map/reduce_scatter | solution.py:36
  595.5 1.6 convert_element_type.21
  (1 shorter events, 0.0 us)
Async XLA Ops:
  7.2 200.0 %reduce-scatter.3.cloned.1.call-start = ((), (), s32[]{:S(2)}) async-start(), calls=%async_computation.3 | async-start | bytes 3932160 | tf_op jit(solution)/shard_map/reduce_scatter | solution.py:30
  7.2 156.8 %slice-start = ((s8[4718592]{0:T(1024)(128)(4,1)}), s8[4194304]{0:T(1024)(128)(4,1)S(1)}, s32[]{:S(2)}) async-start(s8[4718592]{0:T(1024)(128)(4,1)} %bitcast.11), calls=%async_computation.6 | async-start | bytes 8388608
  9.0 154.9 %slice-start.1 = ((s8[4718592]{0:T(1024)(128)(4,1)}), s8[524288]{0:T(1024)(128)(4,1)S(1)}, s32[]{:S(2)}) async-start(s8[4718592]{0:T(1024)(128)(4,1)} %bitcast.11), calls=%async_computation.7 | async-start | bytes 1048576
  161.4 2.6 copy-start
  164.0 43.2 %copy-start.1 = (bf16[256,768]{1,0:T(8,128)(2,1)S(1)}, bf16[256,768]{1,0:T(8,128)(2,1)}, u32[]{:S(2)}) copy-start(bf16[256,768]{1,0:T(8,128)(2,1)} %param.5) | copy-start | bytes 1179652
  170.7 68.4 %all-gather.2.cloned.1.call-start = ((), (), s32[]{:S(2)}) async-start(), calls=%async_computation.4 | async-start | bytes 1966080 | tf_op jit(solution)/shard_map/all_gather | solution.py:32
  209.8 385.7 %reduce-scatter.5.cloned.1.call-start = ((), (), s32[]{:S(2)}) async-start(), calls=%async_computation.5 | async-start | bytes 12779520 | tf_op jit(solution)/shard_map/reduce_scatter | solution.py:36
  249.2 1.4 copy-start.2
Sparse Core Ops, SparseCore 0:
  170.8 36.3 reduce-scatter.2
  209.9 29.1 all-gather.1
  249.3 346.1 reduce-scatter.4
